TPU v7x, 32 devices: a whole 2x2x4 slice. The times are simulated.
32 devices in a mesh: brick: 8 (over y, x, core), chan: 4 (over z).
Axes of the slice: x: 2, y: 2, z: 4, core: 2. Of those that a mesh axis runs over, the one named last changes fastest.
Arguments:
- node_x: bfloat16 [49, 128, 1024], P(None, 'chan', 'brick'), may hold values from -6 to 6
- cotangent: bfloat16 [49, 128, 1024], P(None, 'chan', 'brick'), may hold values from -6 to 6
- wigner: bfloat16 [235, 8192], P(None, 'brick'), may hold values from -4 to 4
- src_index: int32 [8192], P('brick'), may hold values from 0 to 191
- dst_index: int32 [8192], P('brick'), may hold values from 0 to 127
- edge_scale: float32 [8192], P('brick'), may hold values from 0.1 to 1
- edge_count: int32 [8], P('brick'), may hold values from 341 to 1024, as said below
- w_zero: bfloat16 [7, 128, 7, 128], P(None, 'chan'), may hold values from -0.1875 to 0.1875
- w_one: bfloat16 [2, 6, 128, 6, 128], P(None, None, 'chan'), may hold values from -0.15625 to 0.15625
- w_two: bfloat16 [2, 5, 128, 5, 128], P(None, None, 'chan'), may hold values from -0.15625 to 0.15625
Outputs:
- grad_x: float32 [49, 128, 1024], P(None, 'chan', 'brick')
- grad_w_zero: float32 [7, 128, 7, 128], P(None, 'chan', None, 'brick')
- grad_w_one: float32 [2, 6, 128, 6, 128], P(None, None, 'chan', None, 'brick')
- grad_w_two: float32 [2, 5, 128, 5, 128], P(None, None, 'chan', None, 'brick')
Inputs may be any that keep to these rules, and one draw needn't show every extreme that they name: Slots 0 to edge_count[b] - 1 of brick b hold edges, the rest are padding; one brick's list is full.
All inputs are finite; a program needn't handle non-finite values.
Results may differ from a plain program's by a relative error of at most 0.0065.
Values may be sent and summed in bfloat16 or wider, within the bound.
A program may use at most 64 MiB of HBM per device.

v0:
```python
import functools

import jax
import jax.numpy as jnp
from jax import lax
from jax.experimental import pallas as pl
from jax.experimental.pallas import tpu as pltpu
from jax.sharding import PartitionSpec as P

LANES = 128
VMEM_BYTES = 48 * 1024 * 1024
MESH = pl.DeviceIdType.MESH
NT = (((1,), (1,)), ((), ()))
NN = (((1,), (0,)), ((), ()))


def degree_offset(degree):
    return sum((2 * min(k, 2) + 1) * (2 * k + 1) for k in range(degree))


def rotate_tile(load, wig, store):
    for degree in range(7):
        top = min(degree, 2)
        span = 2 * degree + 1
        offset = degree_offset(degree)
        sums = [None] * (2 * top + 1)
        for column in range(span):
            value = load(degree * degree + column)
            for m in range(2 * top + 1):
                term = wig(offset + m * span + column) * value
                sums[m] = term if sums[m] is None else sums[m] + term
        for m in range(2 * top + 1):
            store(kept_row(degree, m - top), sums[m])


def unrotate_tile(load, wig, store):
    for degree in range(7):
        top = min(degree, 2)
        span = 2 * degree + 1
        offset = degree_offset(degree)
        rows = [load(kept_row(degree, m - top)) for m in range(2 * top + 1)]
        for column in range(span):
            total = None
            for m in range(2 * top + 1):
                term = wig(offset + m * span + column) * rows[m]
                total = term if total is None else total + term
            store(degree * degree + column, total)


def source_onehot(src, rows, rim):
    place = jnp.where(src < rim, src + (rows - rim), src - rim)
    return (lax.broadcasted_iota(jnp.int32, (rows, src.shape[1]), 0) == place).astype(jnp.bfloat16)


def dot(a, b, dims):
    return lax.dot_general(a, b, dims, preferred_element_type=jnp.float32)


def fused_kernel(
    bricks, shards, chan, total, piece, rim, width,
    count_ref, src_ref, dst_ref, scale_ref, wig_ref, cot_ref, x_ref, wz_ref, w1_ref, w2_ref,
    sum_ref, gx_ref,
    wide, scaled, at_dst, at_src, cot, x_next, x_prev, ext, gathered, grad, edge_in,
    wz, w1, w2, back, full, gx, part, near, far, outgoing, to_next, to_prev, from_next, from_prev,
    send_up, send_down, recv_cot, send_x, recv_x, send1, recv1, send2, recv2, send_rim, recv_rim,
):
    me = lax.axis_index("brick")
    z = lax.axis_index("chan")
    core = lax.rem(me, 2)
    mine = lax.div(me, 2)
    pairs = bricks // 2
    sibling = me + 1 - 2 * core
    following = lax.rem(me + 1, bricks)
    previous = lax.rem(me + bricks - 1, bricks)
    atoms = x_ref.shape[1]
    slots = src_ref.shape[1]
    coef = x_ref.shape[0] // chan
    f32, bf16 = jnp.float32, jnp.bfloat16

    barrier = pltpu.get_barrier_semaphore()
    for d in range(1, bricks):
        pl.semaphore_signal(
            barrier, inc=1, device_id={"brick": lax.rem(me + d, bricks)}, device_id_type=MESH
        )

    @pl.when(z > 0)
    def _():
        pl.semaphore_signal(barrier, inc=1, device_id={"chan": z - 1}, device_id_type=MESH)

    @pl.when(z < shards - 1)
    def _():
        pl.semaphore_signal(barrier, inc=1, device_id={"chan": z + 1}, device_id_type=MESH)

    ends = jnp.where(z > 0, 1, 0) + jnp.where(z < shards - 1, 1, 0)
    pl.semaphore_wait(barrier, bricks - 1 + ends)

    def remote(src, dst, send, recv, axis, to):
        return pltpu.make_async_remote_copy(
            src_ref=src, dst_ref=dst, send_sem=send, recv_sem=recv,
            device_id={axis: to}, device_id_type=MESH,
        )

    def up(s, src=None):
        src = cot.at[s] if src is None else src
        return remote(src, cot.at[s], send_up.at[s], recv_cot.at[s], "chan", z + 1)

    def down(s, src=None):
        src = cot.at[s] if src is None else src
        return remote(src, cot.at[s], send_down.at[s], recv_cot.at[s], "chan", z - 1)

    @pl.when(z < shards - 1)
    def _():
        up(z, cot_ref).start()

    @pl.when(z > 0)
    def _():
        down(z, cot_ref).start()

    halos = [
        remote(x_ref, x_next, send_x.at[0], recv_x.at[0], "brick", previous),
        remote(x_ref, x_prev, send_x.at[1], recv_x.at[1], "brick", following),
    ]
    for copy in halos:
        copy.start()

    cot[z] = cot_ref[...]
    position = lax.broadcasted_iota(jnp.int32, (1, slots), 1)
    factor = jnp.where(position < count_ref[0], 0.25 * scale_ref[...], 0.0)
    wide[...] = wig_ref[...].astype(f32)
    scaled[...] = wide[...] * factor
    at_dst[...] = (
        lax.broadcasted_iota(jnp.int32, (atoms, slots), 0) == dst_ref[...]
    ).astype(bf16)
    at_src[...] = source_onehot(src_ref[...], 2 * atoms, rim)
    for kept, source, high in (
        (wz, wz_ref, 7), (w1.at[0], w1_ref.at[0], 6), (w1.at[1], w1_ref.at[1], 6),
        (w2.at[0], w2_ref.at[0], 5), (w2.at[1], w2_ref.at[1], 5),
    ):
        for i in range(high):
            for j in range(high):
                kept[i * chan : (i + 1) * chan, j * total : (j + 1) * total] = source[i, j]

    def rotate_all(values, onehot, entries, out, stride, first):
        def block_step(i, carry):
            cols = pl.ds(pl.multiple_of(i * width, width), width)
            gathered[...] = dot(values(), onehot[:, cols], NN)

            def lanes_step(t, inner):
                near_at = pl.ds(pl.multiple_of(t * LANES, LANES), LANES)
                at = pl.ds(pl.multiple_of(i * width + t * LANES, LANES), LANES)

                def store(row, tile):
                    out[pl.ds(pl.multiple_of(row * stride + first, chan), chan), at] = tile.astype(
                        bf16
                    )

                rotate_tile(
                    lambda c: gathered[c * chan : (c + 1) * chan, near_at],
                    lambda k: entries[k : k + 1, at],
                    store,
                )
                return inner

            lax.fori_loop(0, width // LANES, lanes_step, 0)
            return carry

        lax.fori_loop(0, slots // width, block_step, 0)

    lane = lax.broadcasted_iota(jnp.int32, (1, atoms), 1)

    def distance_step(d, carry):
        low, high = z - d, z + d

        @pl.when((d > 0) & (low >= 0))
        def _():
            down_in = remote(cot_ref, cot.at[low], send_up.at[low], recv_cot.at[low], "chan", z)
            down_in.wait_recv()

            @pl.when(z < shards - 1)
            def _():
                up(low).start()

        @pl.when((d > 0) & (high < shards))
        def _():
            up_in = remote(cot_ref, cot.at[high], send_up.at[high], recv_cot.at[high], "chan", z)
            up_in.wait_recv()

            @pl.when(z > 0)
            def _():
                down(high).start()

        def side_step(side, inner):
            s = jnp.where(side == 0, low, high)

            @pl.when((s >= 0) & (s < shards) & (d + (1 - side) > 0))
            def _():
                rotate_all(lambda: cot[s], at_dst, scaled, grad, total, s * chan)

            return inner

        lax.fori_loop(0, 2, side_step, 0)

        @pl.when(d == 0)
        def _():
            for copy in halos:
                copy.wait_recv()
            ext[:, :atoms] = x_ref[...]
            ext[:, atoms:] = jnp.where(
                lane < rim, x_next[...].astype(f32), x_prev[...].astype(f32)
            ).astype(bf16)
            rotate_all(lambda: ext[...], at_src, wide, edge_in, chan, 0)

        return carry

    lax.fori_loop(0, shards, distance_step, 0)

    def split(row, high, value):
        for c in range(bricks):
            for j in range(high):
                lines = value[j * total + c * piece : j * total + (c + 1) * piece]
                part[c, row + j * piece : row + (j + 1) * piece, : high * chan] = lines.astype(bf16)

    part[...] = jnp.zeros_like(part)
    split(0, 7, dot(grad[: 7 * total], edge_in[: 7 * chan], NT))
    row = 7 * piece
    for first, high in ((7, 6), (19, 5)):
        grad_plus = grad[first * total : (first + high) * total]
        grad_minus = grad[(first + high) * total : (first + 2 * high) * total]
        in_plus = edge_in[first * chan : (first + high) * chan]
        in_minus = edge_in[(first + high) * chan : (first + 2 * high) * chan]
        split(row, high, dot(grad_plus, in_plus, NT) + dot(grad_minus, in_minus, NT))
        row += high * piece
        split(row, high, dot(grad_minus, in_plus, NT) - dot(grad_plus, in_minus, NT))
        row += high * piece

    order = [d for d in range(pairs - 1, 0, -1)] + [0]
    stage_one = []
    for d in order:
        q = lax.rem(mine + d, pairs)
        copy = remote(
            part.at[2 * q + (1 - core)], near.at[d], send1.at[d], recv1.at[d], "brick", sibling
        )
        copy.start()
        stage_one.append(copy)

    gx[...] = jnp.zeros_like(gx)

    def back_block(i, carry):
        cols = pl.ds(pl.multiple_of(i * width, width), width)
        back[: 7 * chan] = dot(wz[...], grad[: 7 * total, cols], NN)
        for w, first, high in ((w1, 7, 6), (w2, 19, 5)):
            low, middle, top = first, first + high, first + 2 * high
            plus = grad[low * total : middle * total, cols]
            minus = grad[middle * total : top * total, cols]
            back[low * chan : middle * chan] = dot(w[0], plus, NN) + dot(w[1], minus, NN)
            back[middle * chan : top * chan] = dot(w[0], minus, NN) - dot(w[1], plus, NN)

        def lanes_step(t, inner):
            near_at = pl.ds(pl.multiple_of(t * LANES, LANES), LANES)
            at = pl.ds(pl.multiple_of(i * width + t * LANES, LANES), LANES)

            def store(c, tile):
                full[c * chan : (c + 1) * chan, near_at] = tile.astype(bf16)

            unrotate_tile(
                lambda r: back[r * chan : (r + 1) * chan, near_at],
                lambda k: wide[k : k + 1, at],
                store,
            )
            return inner

        lax.fori_loop(0, width // LANES, lanes_step, 0)
        gx[: coef * chan] += dot(full[...], at_src[:, cols], NT)
        return carry

    lax.fori_loop(0, 1, back_block, 0)
    stage_two = []
    for copy, d in zip(stage_one, order):
        copy.wait_recv()
        q = lax.rem(mine + d, pairs)
        both = part[2 * q + core].astype(f32) + near[d].astype(f32)
        if d:
            outgoing[d] = both.astype(bf16)
            copy = remote(
                outgoing.at[d], far.at[d], send2.at[d], recv2.at[d], "brick", 2 * q + core
            )
            copy.start()
            stage_two.append(copy)
        else:
            sum_ref[...] = both
    lax.fori_loop(1, slots // width, back_block, 0)

    groups = atoms // rim
    rows = chan // groups
    tile = gx[:, atoms:].reshape(coef + 1, chan, atoms)
    for packed, start in ((to_next, 0), (to_prev, atoms - rim)):
        laid = jnp.zeros((coef + 1, rows, atoms), f32)
        for q in range(groups):
            turn = (q * rim - start) % atoms
            lines = tile[:, q * rows : (q + 1) * rows].reshape(-1, atoms)
            lines = pltpu.roll(lines, turn, 1) if turn else lines
            inside = (lane >= q * rim) & (lane < (q + 1) * rim)
            laid = jnp.where(inside[None], lines.reshape(laid.shape), laid)
        packed[...] = laid.reshape(packed.shape).astype(bf16)
    rims = [
        remote(to_next, from_prev, send_rim.at[0], recv_rim.at[0], "brick", following),
        remote(to_prev, from_next, send_rim.at[1], recv_rim.at[1], "brick", previous),
    ]
    for copy in rims:
        copy.start()
    for copy, d in zip(stage_two, order):
        copy.wait_recv()
        sum_ref[...] += far[d].astype(f32)
    for copy in rims:
        copy.wait_recv()
    arrived = [from_prev[...].astype(f32), from_next[...].astype(f32)]
    for q in range(groups):
        total_lines = gx[: coef * chan, :atoms].reshape(coef, chan, atoms)[
            :, q * rows : (q + 1) * rows
        ]
        for lines, start in zip(arrived, (0, atoms - rim)):
            turn = (start - q * rim) % atoms
            lines = pltpu.roll(lines, turn, 1) if turn else lines
            inside = (lane >= start) & (lane < start + rim)
            lines = jnp.where(inside, lines, 0.0)
            total_lines = total_lines + lines.reshape(coef + 1, rows, atoms)[:coef]
        gx_ref[:, q * rows : (q + 1) * rows, :] = total_lines

    for copy in halos + stage_one + stage_two + rims:
        copy.wait_send()
    for s in range(shards):
        @pl.when((z < shards - 1) & (s <= z))
        def _():
            up(s).wait_send()

        @pl.when((z > 0) & (s >= z))
        def _():
            down(s).wait_send()


def kernel_body(
    node_x, cotangent, wigner, src_index, dst_index, edge_scale, edge_count, w_zero, w_one, w_two
):
    bricks, shards = lax.axis_size("brick"), lax.axis_size("chan")
    coef, chan, atoms = node_x.shape
    total = w_zero.shape[3]
    piece = total // bricks
    rim = atoms // 4
    slots = src_index.shape[0]
    entries = wigner.shape[0]
    width = 256
    f32, bf16 = jnp.float32, jnp.bfloat16
    pairs = bricks // 2
    rows = (7 + 12 + 10) * piece
    flat = coef * chan
    packed = (coef + 1) * (chan * rim // atoms)

    def vmem(shape, dtype):
        return pltpu.VMEM(shape, dtype)

    def dma(count):
        return pltpu.SemaphoreType.DMA((count,))

    whole = pl.BlockSpec(memory_space=pltpu.VMEM)
    sums, grad_x = pl.pallas_call(
        functools.partial(fused_kernel, bricks, shards, chan, total, piece, rim, width),
        out_shape=(
            jax.ShapeDtypeStruct((rows, 2 * LANES), f32),
            jax.ShapeDtypeStruct((coef, chan, atoms), f32),
        ),
        in_specs=[pl.BlockSpec(memory_space=pltpu.SMEM)] + [whole] * 9,
        out_specs=(whole, whole),
        scratch_shapes=[
            vmem((entries, slots), f32), vmem((entries, slots), f32),
            vmem((atoms, slots), bf16), vmem((2 * atoms, slots), bf16),
            vmem((shards, flat, atoms), bf16), vmem((flat, atoms), bf16),
            vmem((flat, atoms), bf16), vmem((flat, 2 * atoms), bf16),
            vmem((flat, width), f32), vmem((29 * total, slots), bf16),
            vmem((29 * chan, slots), bf16), vmem((7 * chan, 7 * total), bf16),
            vmem((2, 6 * chan, 6 * total), bf16), vmem((2, 5 * chan, 5 * total), bf16),
            vmem((29 * chan, width), f32), vmem((flat, width), bf16),
            vmem((flat + chan, 2 * atoms), f32), vmem((bricks, rows, 2 * LANES), bf16),
            vmem((pairs, rows, 2 * LANES), bf16), vmem((pairs, rows, 2 * LANES), bf16),
            vmem((pairs, rows, 2 * LANES), bf16),
            vmem((packed, atoms), bf16), vmem((packed, atoms), bf16),
            vmem((packed, atoms), bf16), vmem((packed, atoms), bf16),
            dma(shards), dma(shards), dma(shards), dma(2), dma(2),
            dma(pairs), dma(pairs), dma(pairs), dma(pairs), dma(2), dma(2),
        ],
        compiler_params=pltpu.CompilerParams(
            vmem_limit_bytes=VMEM_BYTES, collective_id=0, has_side_effects=True
        ),
        name="fused",
    )(
        edge_count, src_index.reshape(1, slots), dst_index.reshape(1, slots),
        edge_scale.reshape(1, slots), wigner, cotangent.reshape(flat, atoms),
        node_x.reshape(flat, atoms), w_zero.transpose(0, 2, 1, 3),
        w_one.transpose(0, 1, 3, 2, 4), w_two.transpose(0, 1, 3, 2, 4),
    )

    def columns_back(first, high):
        block = sums[first : first + high * piece, : high * chan]
        return block.reshape(high, piece, high, chan).transpose(2, 3, 0, 1)

    ends = [0, 7 * piece, 13 * piece, 19 * piece, 24 * piece]
    return (
        grad_x,
        columns_back(ends[0], 7),
        jnp.stack([columns_back(ends[1], 6), columns_back(ends[2], 6)]),
        jnp.stack([columns_back(ends[3], 5), columns_back(ends[4], 5)]),
    )


def padded(x, sides, width):
    for axis, dim in sides:
        devices, length = (lax.axis_size(axis), x.shape[dim])
        up = [(i, (i + 1) % devices) for i in range(devices)]
        down = [(j, i) for i, j in up]
        last = lax.slice_in_dim(x, length - width, length, axis=dim)
        initial = lax.slice_in_dim(x, 0, width, axis=dim)
        before = lax.ppermute(last, axis, up)
        after = lax.ppermute(initial, axis, down)
        x = jnp.concatenate([before, x, after], axis=dim)
    return x


def passed_along(block, axis, distance):
    devices = range(lax.axis_size(axis))
    route = [((i - distance) % len(devices), i) for i in devices]
    return lax.ppermute(block, axis, route)


def kept_row(degree, azimuth):
    if azimuth == 0:
        return degree
    if azimuth == 1:
        return 6 + degree
    if azimuth == -1:
        return 12 + degree
    if azimuth == 2:
        return 17 + degree
    return 22 + degree


def to_edge_frame(values, wigner):
    kept_rows = [None] * 29
    offset = 0
    for degree in range(7):
        max_order = min(degree, 2)
        span_cols = 2 * degree + 1
        for azimuth in range(-max_order, max_order + 1):
            running = jnp.zeros(values.shape[1:], jnp.float32)
            for column in range(span_cols):
                factor = wigner[offset + (azimuth + max_order) * span_cols + column].astype(
                    jnp.float32
                )
                running = running + factor[None, :] * values[degree * degree + column].astype(
                    jnp.float32
                )
            kept_rows[kept_row(degree, azimuth)] = running
        offset += (2 * max_order + 1) * span_cols
    return jnp.stack(kept_rows)


def from_edge_frame(kept_rows, wigner):
    full_rows = []
    offset = 0
    for degree in range(7):
        max_order = min(degree, 2)
        span_cols = 2 * degree + 1
        for column in range(span_cols):
            running = jnp.zeros(kept_rows.shape[1:], jnp.float32)
            for azimuth in range(-max_order, max_order + 1):
                factor = wigner[offset + (azimuth + max_order) * span_cols + column].astype(
                    jnp.float32
                )
                running = running + factor[None, :] * kept_rows[kept_row(degree, azimuth)]
            full_rows.append(running)
        offset += (2 * max_order + 1) * span_cols
    return jnp.stack(full_rows)


def contract(weights, grads):
    return lax.dot_general(
        weights, grads, (((2, 3), (0, 1)), ((), ())), preferred_element_type=jnp.float32
    )


def outer(inputs, grads):
    return lax.dot_general(
        inputs, grads, (((2,), (2,)), ((), ())), preferred_element_type=jnp.float32
    )


def so2_back(w_zero, w_one, w_two, edge_grad, edge_in):
    back_rows = [contract(w_zero, edge_grad[0:7])]
    term_zero = outer(edge_in[0:7], edge_grad[0:7])
    weight_terms = []
    for weights, bottom, middle, ceiling in ((w_one, 7, 13, 19), (w_two, 19, 24, 29)):
        grad_plus = edge_grad[bottom:middle]
        grad_minus = edge_grad[middle:ceiling]
        in_plus = edge_in[bottom:middle]
        in_minus = edge_in[middle:ceiling]
        back_rows.append(contract(weights[0], grad_plus) + contract(weights[1], grad_minus))
        back_rows.append(contract(weights[0], grad_minus) - contract(weights[1], grad_plus))
        weight_terms.append(
            jnp.stack(
                [
                    outer(in_plus, grad_plus) + outer(in_minus, grad_minus),
                    outer(in_plus, grad_minus) - outer(in_minus, grad_plus),
                ]
            )
        )
    return (jnp.concatenate(back_rows, axis=0), term_zero, weight_terms[0], weight_terms[1])


def add_columns(summed, term, first_col, axis_dim):
    current = lax.dynamic_slice_in_dim(summed, first_col, term.shape[axis_dim], axis_dim)
    return lax.dynamic_update_slice_in_dim(summed, current + term, first_col, axis_dim)


def body(
    node_x, cotangent, wigner, src_index, dst_index, edge_scale, edge_count, w_zero, w_one, w_two
):
    atom_count = node_x.shape[2]
    own_chan = node_x.shape[1]
    coef_count = node_x.shape[0]
    chan_total = w_zero.shape[3]
    rim_len = atom_count // 4
    slot_count = src_index.shape[0]
    block_len = min(512, slot_count)
    live_count = edge_count[0]
    padded_len = atom_count + 2 * rim_len
    extended = padded(node_x, (("brick", 2),), rim_len)
    at_source = jnp.take(extended, src_index, axis=2)
    edge_in = to_edge_frame(at_source, wigner).astype(jnp.bfloat16)
    block_total = slot_count // block_len
    initial = (
        jnp.zeros((29, own_chan, slot_count), jnp.float32),
        jnp.zeros(w_zero.shape[:3] + (chan_total,), jnp.float32),
        jnp.zeros(w_one.shape[:4] + (chan_total,), jnp.float32),
        jnp.zeros(w_two.shape[:4] + (chan_total,), jnp.float32),
    )
    full_grad = lax.all_gather(cotangent, "chan", axis=1, tiled=True)

    def block_step(block_index, running):
        edge_back, sum_zero, sum_one, sum_two = running
        begin_at = block_index * block_len
        dst_block = lax.dynamic_slice_in_dim(dst_index, begin_at, block_len)
        wig_block = lax.dynamic_slice_in_dim(wigner, begin_at, block_len, 1)
        scale_block = lax.dynamic_slice_in_dim(edge_scale, begin_at, block_len)
        position = begin_at + lax.iota(jnp.int32, block_len)
        factor = jnp.where(position < live_count, 0.25 * scale_block, 0.0)
        at_dest = jnp.take(full_grad, dst_block, axis=2)
        edge_grad = (to_edge_frame(at_dest, wig_block) * factor).astype(jnp.bfloat16)
        edge_block = lax.dynamic_slice_in_dim(edge_in, begin_at, block_len, 2)
        back_rows, term_zero, term_one, term_two = so2_back(
            w_zero, w_one, w_two, edge_grad, edge_block
        )
        edge_back = add_columns(edge_back, back_rows, begin_at, 2)
        sum_zero = add_columns(sum_zero, term_zero, 0, 3)
        sum_one = add_columns(sum_one, term_one, 0, 4)
        sum_two = add_columns(sum_two, term_two, 0, 4)
        return (edge_back, sum_zero, sum_one, sum_two)

    folded = lax.fori_loop(0, block_total, block_step, initial)
    edge_back, sum_zero, sum_one, sum_two = folded

    def back_step(block_index, summed):
        begin_at = block_index * block_len
        kept_rows = lax.dynamic_slice_in_dim(edge_back, begin_at, block_len, 2)
        wig_block = lax.dynamic_slice_in_dim(wigner, begin_at, block_len, 1)
        src_block = lax.dynamic_slice_in_dim(src_index, begin_at, block_len)
        full_rows = from_edge_frame(kept_rows, wig_block)
        onehot = (src_block[:, None] == lax.iota(jnp.int32, padded_len)[None, :]).astype(
            jnp.bfloat16
        )
        high_part = full_rows.astype(jnp.bfloat16)
        rest = full_rows - high_part.astype(jnp.float32)
        low_part = rest.astype(jnp.bfloat16)
        dims = (((2,), (0,)), ((), ()))
        summed = summed + lax.dot_general(
            high_part, onehot, dims, preferred_element_type=jnp.float32
        )
        return summed + lax.dot_general(low_part, onehot, dims, preferred_element_type=jnp.float32)

    grad_ext = lax.fori_loop(
        0, block_total, back_step, jnp.zeros((coef_count, own_chan, padded_len), jnp.float32)
    )
    own_part = grad_ext[:, :, rim_len : rim_len + atom_count]
    from_above = passed_along(grad_ext[:, :, :rim_len], "brick", -1)
    from_below = passed_along(grad_ext[:, :, rim_len + atom_count :], "brick", 1)
    own_part = own_part.at[:, :, :rim_len].add(from_below)
    grad_x = own_part.at[:, :, atom_count - rim_len :].add(from_above)
    return (
        grad_x,
        lax.psum_scatter(sum_zero, "brick", scatter_dimension=3, tiled=True),
        lax.psum_scatter(
            sum_one.reshape((-1,) + sum_one.shape[2:]), "brick", scatter_dimension=3, tiled=True
        ).reshape(sum_one.shape[:4] + (-1,)),
        lax.psum_scatter(
            sum_two.reshape((-1,) + sum_two.shape[2:]), "brick", scatter_dimension=3, tiled=True
        ).reshape(sum_two.shape[:4] + (-1,)),
    )


def solution(mesh):
    in_specs = (
        P(None, "chan", "brick"),
        P(None, "chan", "brick"),
        P(None, "brick"),
        P("brick"),
        P("brick"),
        P("brick"),
        P("brick"),
        P(None, "chan", None, None),
        P(None, None, "chan", None, None),
        P(None, None, "chan", None, None),
    )
    out_specs = (
        P(None, "chan", "brick"),
        P(None, "chan", None, "brick"),
        P(None, None, "chan", None, "brick"),
        P(None, None, "chan", None, "brick"),
    )
    bricks, shards = mesh.shape["brick"], mesh.shape["chan"]
    fits = bricks % 2 == 0 and bricks > 2 and (128 // bricks) % 16 == 0 and shards <= 4
    chosen = kernel_body if fits else body
    return jax.shard_map(chosen, mesh=mesh, in_specs=in_specs, out_specs=out_specs, check_vma=False)
```

profile of v0, /device:TPU:0, one launch (start us, length us, event | category | flops | bytes accessed | tf_op | source)
XLA Modules:
  0.0 76.7 jit_solution(8216502740632873584)
XLA Ops:
  1.3 0.0 copy-start.8
  1.3 0.0 copy-start.7
  1.3 0.0 copy-start.6
  1.3 0.7 copy-done.8
  2.0 0.0 copy-done.7
  2.0 0.0 copy-done.6
  2.0 0.0 copy-start
  2.0 1.1 %copy-done = bf16[2,6,32,6,128]{4,2,3,1,0:T(8,128)(2,1)S(1)} copy-done((bf16[2,6,32,6,128]{4,2,3,1,0:T(8,128)(2,1)S(1)}, bf16[2,6,32,6,128]{4,2,3,1,0:T(8,128)(2,1)}, u32[]{:S(2)}) %copy-start) | copy-done | bytes 589848
  3.1 0.0 copy-start.1
  3.1 1.0 %copy-done.1 = bf16[235,1024]{1,0:T(8,128)(2,1)S(1)} copy-done((bf16[235,1024]{1,0:T(8,128)(2,1)S(1)}, bf16[235,1024]{1,0:T(8,128)(2,1)}, u32[]{:S(2)}) %copy-start.1) | copy-done | bytes 481304
  4.1 0.0 copy-start.2
  4.1 1.0 %copy-done.2 = bf16[2,5,32,5,128]{4,2,3,1,0:T(8,128)(2,1)S(1)} copy-done((bf16[2,5,32,5,128]{4,2,3,1,0:T(8,128)(2,1)S(1)}, bf16[2,5,32,5,128]{4,2,3,1,0:T(8,128)(2,1)}, u32[]{:S(2)}) %copy-start.2) | copy-done | bytes 409624
  5.1 0.0 copy-start.3
  5.1 1.0 %copy-done.3 = bf16[49,32,128]{2,1,0:T(8,128)(2,1)S(1)} copy-done((bf16[49,32,128]{2,1,0:T(8,128)(2,1)S(1)}, bf16[49,32,128]{2,1,0:T(8,128)(2,1)}, u32[]{:S(2)}) %copy-start.3) | copy-done | bytes 401432
  6.1 0.0 copy-start.4
  6.1 1.0 %copy-done.4 = bf16[49,32,128]{2,1,0:T(8,128)(2,1)S(1)} copy-done((bf16[49,32,128]{2,1,0:T(8,128)(2,1)S(1)}, bf16[49,32,128]{2,1,0:T(8,128)(2,1)}, u32[]{:S(2)}) %copy-start.4) | copy-done | bytes 401432
  7.1 0.0 copy-start.5
  7.1 1.0 %copy-done.5 = bf16[7,32,7,128]{3,1,2,0:T(8,128)(2,1)S(1)} copy-done((bf16[7,32,7,128]{3,1,2,0:T(8,128)(2,1)S(1)}, bf16[7,32,7,128]{3,1,2,0:T(8,128)(2,1)}, u32[]{:S(2)}) %copy-start.5) | copy-done | bytes 401432
  8.1 64.2 %fused.1 = (f32[464,256]{1,0:T(8,128)S(1)}, f32[49,32,128]{2,1,0:T(8,128)S(1)}) custom-call(s32[1]{0:T(128)S(6)} %copy.23.count_ref, s32[1,1024]{1,0:T(1,128)S(1)} %bitcast.26, s32[1,1024]{1,0:T(1,128)S(1)} %bitcast.27, f32[1,1024]{1,0:T(1,128)S(1)} %bitcast.28, bf16[235,1024]{1,0:T(8,128)(2,1)S(1)} %copy-done.1, bf16[1568,128]{1,0:T(8,128)(2,1)S(1)} %bitcast.23, ...), custom_call_target="tpu_custom_call" | custom-call | tf_op jit(solution)/shard_map/fused/pallas_call | solution.py:365
  72.4 0.1 reshape.44
  72.5 0.1 reshape.45
  72.6 0.1 pad_maximum_fusion
  72.7 0.9 %copy.20 = f32[2,6,32,6,16]{2,4,3,1,0:T(8,128)} copy(f32[2,6,32,6,16]{2,1,4,3,0:T(8,128)S(1)} %pad_maximum_fusion) | data formatting | bytes 294912
  73.7 0.1 reshape.46
  73.8 0.1 reshape.47
  73.9 0.1 pad_maximum_fusion.1
  74.0 0.8 %copy.21 = f32[2,5,32,5,16]{2,4,3,1,0:T(8,128)} copy(f32[2,5,32,5,16]{2,1,4,3,0:T(8,128)S(1)} %pad_maximum_fusion.1) | data formatting | bytes 204800
  74.8 0.1 reshape.43
  75.0 0.8 %copy.19 = f32[7,32,7,16]{1,3,2,0:T(8,128)} copy(f32[7,32,7,16]{1,0,3,2:T(8,128)S(1)} %bitcast.29) | data formatting | bytes 200704
  75.8 0.9 %copy.24 = f32[49,32,128]{2,1,0:T(8,128)} copy(f32[49,32,128]{2,1,0:T(8,128)S(1)} %get-tuple-element.20) | data formatting | bytes 1605632
  (3 shorter events, 0.0 us)
Async XLA Ops:
  1.3 0.7 copy-start.8
  1.3 0.7 copy-start.7
  1.3 0.7 copy-start.6
  2.0 1.1 %copy-start = (bf16[2,6,32,6,128]{4,2,3,1,0:T(8,128)(2,1)S(1)}, bf16[2,6,32,6,128]{4,2,3,1,0:T(8,128)(2,1)}, u32[]{:S(2)}) copy-start(bf16[2,6,32,6,128]{4,2,3,1,0:T(8,128)(2,1)} %param.18) | copy-start | bytes 1769476
  3.1 1.0 %copy-start.1 = (bf16[235,1024]{1,0:T(8,128)(2,1)S(1)}, bf16[235,1024]{1,0:T(8,128)(2,1)}, u32[]{:S(2)}) copy-start(bf16[235,1024]{1,0:T(8,128)(2,1)} %wig_ref.1) | copy-start | bytes 1443844
  4.1 1.0 %copy-start.2 = (bf16[2,5,32,5,128]{4,2,3,1,0:T(8,128)(2,1)S(1)}, bf16[2,5,32,5,128]{4,2,3,1,0:T(8,128)(2,1)}, u32[]{:S(2)}) copy-start(bf16[2,5,32,5,128]{4,2,3,1,0:T(8,128)(2,1)} %param.19) | copy-start | bytes 1228804
  5.1 1.0 %copy-start.3 = (bf16[49,32,128]{2,1,0:T(8,128)(2,1)S(1)}, bf16[49,32,128]{2,1,0:T(8,128)(2,1)}, u32[]{:S(2)}) copy-start(bf16[49,32,128]{2,1,0:T(8,128)(2,1)} %param.11) | copy-start | bytes 1204228
  6.1 1.0 %copy-start.4 = (bf16[49,32,128]{2,1,0:T(8,128)(2,1)S(1)}, bf16[49,32,128]{2,1,0:T(8,128)(2,1)}, u32[]{:S(2)}) copy-start(bf16[49,32,128]{2,1,0:T(8,128)(2,1)} %param.10) | copy-start | bytes 1204228
  7.1 1.0 %copy-start.5 = (bf16[7,32,7,128]{3,1,2,0:T(8,128)(2,1)S(1)}, bf16[7,32,7,128]{3,1,2,0:T(8,128)(2,1)}, u32[]{:S(2)}) copy-start(bf16[7,32,7,128]{3,1,2,0:T(8,128)(2,1)} %param.17) | copy-start | bytes 1204228
where the time goes:
time: 77.1 us; the launch traced here: 76.7 us
  Pallas kernels  64.2 us (83%)
  local copies, waits for them, and re-layouts  10.9 us (14%)
  between operations  1.39 us (2%)
    pallas_call x1, Pallas kernels, kernel_body(): pl.pallas_call(functools.partial(fused_kernel, bricks, shards, chan, tota...  64.2 us
    unnamed x22, local copies, waits for them, and re-layouts  10.3 us

commit v1 on v0

--- a/solution.py
+++ b/solution.py
@@ -60,9 +60,11 @@
     bricks, shards, chan, total, piece, rim, width,
     count_ref, src_ref, dst_ref, scale_ref, wig_ref, cot_ref, x_ref, wz_ref, w1_ref, w2_ref,
     sum_ref, gx_ref,
+    wig_in, wz_in, w1_in, w2_in,
     wide, scaled, at_dst, at_src, cot, x_next, x_prev, ext, gathered, grad, edge_in,
     wz, w1, w2, back, full, gx, part, near, far, outgoing, to_next, to_prev, from_next, from_prev,
-    send_up, send_down, recv_cot, send_x, recv_x, send1, recv1, send2, recv2, send_rim, recv_rim,
+    local, send_up, send_down, recv_cot, send_x, recv_x, send1, recv1, send2, recv2,
+    send_rim, recv_rim,
 ):
     me = lax.axis_index("brick")
     z = lax.axis_index("chan")
@@ -74,6 +76,15 @@
     previous = lax.rem(me + bricks - 1, bricks)
     atoms = x_ref.shape[1]
     slots = src_ref.shape[1]
+    copies = [
+        pltpu.make_async_copy(source, target, local.at[i])
+        for i, (source, target) in enumerate((
+            (wig_ref, wig_in), (cot_ref, cot.at[z]), (x_ref, ext.at[:, :atoms]),
+            (wz_ref, wz_in), (w1_ref, w1_in), (w2_ref, w2_in),
+        ))
+    ]
+    for copy in copies:
+        copy.start()
     coef = x_ref.shape[0] // chan
     f32, bf16 = jnp.float32, jnp.bfloat16
 
@@ -123,22 +134,17 @@
     for copy in halos:
         copy.start()
 
-    cot[z] = cot_ref[...]
-    position = lax.broadcasted_iota(jnp.int32, (1, slots), 1)
-    factor = jnp.where(position < count_ref[0], 0.25 * scale_ref[...], 0.0)
-    wide[...] = wig_ref[...].astype(f32)
-    scaled[...] = wide[...] * factor
     at_dst[...] = (
         lax.broadcasted_iota(jnp.int32, (atoms, slots), 0) == dst_ref[...]
     ).astype(bf16)
     at_src[...] = source_onehot(src_ref[...], 2 * atoms, rim)
-    for kept, source, high in (
-        (wz, wz_ref, 7), (w1.at[0], w1_ref.at[0], 6), (w1.at[1], w1_ref.at[1], 6),
-        (w2.at[0], w2_ref.at[0], 5), (w2.at[1], w2_ref.at[1], 5),
-    ):
-        for i in range(high):
-            for j in range(high):
-                kept[i * chan : (i + 1) * chan, j * total : (j + 1) * total] = source[i, j]
+    back[...] = jnp.zeros_like(back)
+    position = lax.broadcasted_iota(jnp.int32, (1, slots), 1)
+    factor = jnp.where(position < count_ref[0], 0.25 * scale_ref[...], 0.0)
+    copies[0].wait()
+    wide[...] = wig_in[...].astype(f32)
+    scaled[...] = wide[...] * factor
+    copies[1].wait()
 
     def rotate_all(values, onehot, entries, out, stride, first):
         def block_step(i, carry):
@@ -168,6 +174,84 @@
 
     lane = lax.broadcasted_iota(jnp.int32, (1, atoms), 1)
 
+    def first_shard():
+        for copy in copies[3:]:
+            copy.wait()
+        for kept, source, lead, high in (
+            (wz, wz_in, (), 7), (w1, w1_in, (0,), 6), (w1, w1_in, (1,), 6),
+            (w2, w2_in, (0,), 5), (w2, w2_in, (1,), 5),
+        ):
+            for i in range(high):
+                for j in range(high):
+                    tile = source[lead + (i, j)]
+                    for s in range(shards):
+                        kept[
+                            lead + (s, slice(i * chan, (i + 1) * chan),
+                                    slice(j * chan, (j + 1) * chan))
+                        ] = tile[:, s * chan : (s + 1) * chan]
+        copies[2].wait()
+        for copy in halos:
+            copy.wait_recv()
+        ext[:, atoms:] = jnp.where(
+            lane < rim, x_next[...].astype(f32), x_prev[...].astype(f32)
+        ).astype(bf16)
+        rotate_all(lambda: ext[...], at_src, wide, edge_in, chan, 0)
+        part[...] = jnp.zeros_like(part)
+
+    def stage_one(s):
+        return remote(
+            part.at[2 * s + (1 - core)], near.at[s], send1.at[s], recv1.at[s], "brick", sibling
+        )
+
+    def stage_two(s, d):
+        return remote(
+            outgoing.at[s], far.at[d], send2.at[d], recv2.at[d], "brick", 2 * s + core
+        )
+
+    def shard_products(s):
+        def split(row, high, value):
+            for h in range(2):
+                for j in range(high):
+                    lines = value[j * chan + h * piece : j * chan + (h + 1) * piece]
+                    part[2 * s + h, row + j * piece : row + (j + 1) * piece, : high * chan] = (
+                        lines.astype(bf16)
+                    )
+
+        split(0, 7, dot(grad[: 7 * chan], edge_in[: 7 * chan], NT))
+        row = 7 * piece
+        for first, high in ((7, 6), (19, 5)):
+            low, middle, top = first * chan, (first + high) * chan, (first + 2 * high) * chan
+            grad_plus, grad_minus = grad[low:middle], grad[middle:top]
+            in_plus, in_minus = edge_in[low:middle], edge_in[middle:top]
+            split(row, high, dot(grad_plus, in_plus, NT) + dot(grad_minus, in_minus, NT))
+            row += high * piece
+            split(row, high, dot(grad_minus, in_plus, NT) - dot(grad_plus, in_minus, NT))
+            row += high * piece
+        stage_one(s).start()
+
+        def contract_step(i, carry):
+            cols = pl.ds(pl.multiple_of(i * width, width), width)
+            back[: 7 * chan, cols] += dot(wz[s], grad[: 7 * chan, cols], NN)
+            for w, first, high in ((w1, 7, 6), (w2, 19, 5)):
+                low, middle, top = first * chan, (first + high) * chan, (first + 2 * high) * chan
+                plus, minus = grad[low:middle, cols], grad[middle:top, cols]
+                back[low:middle, cols] += dot(w[0, s], plus, NN) + dot(w[1, s], minus, NN)
+                back[middle:top, cols] += dot(w[0, s], minus, NN) - dot(w[1, s], plus, NN)
+            return carry
+
+        lax.fori_loop(0, slots // width, contract_step, 0)
+        stage_one(s).wait_recv()
+        both = part[2 * s + core].astype(f32) + near[s].astype(f32)
+
+        @pl.when(s == mine)
+        def _():
+            sum_ref[...] = both
+
+        @pl.when(s != mine)
+        def _():
+            outgoing[s] = both.astype(bf16)
+            stage_two(s, lax.rem(s - mine + pairs, pairs)).start()
+
     def distance_step(d, carry):
         low, high = z - d, z + d
 
@@ -194,66 +278,25 @@
 
             @pl.when((s >= 0) & (s < shards) & (d + (1 - side) > 0))
             def _():
-                rotate_all(lambda: cot[s], at_dst, scaled, grad, total, s * chan)
+                rotate_all(lambda: cot[s], at_dst, scaled, grad, chan, 0)
+
+                @pl.when(d == 0)
+                def _():
+                    first_shard()
+
+                shard_products(s)
 
             return inner
 
         lax.fori_loop(0, 2, side_step, 0)
-
-        @pl.when(d == 0)
-        def _():
-            for copy in halos:
-                copy.wait_recv()
-            ext[:, :atoms] = x_ref[...]
-            ext[:, atoms:] = jnp.where(
-                lane < rim, x_next[...].astype(f32), x_prev[...].astype(f32)
-            ).astype(bf16)
-            rotate_all(lambda: ext[...], at_src, wide, edge_in, chan, 0)
-
         return carry
 
     lax.fori_loop(0, shards, distance_step, 0)
-
-    def split(row, high, value):
-        for c in range(bricks):
-            for j in range(high):
-                lines = value[j * total + c * piece : j * total + (c + 1) * piece]
-                part[c, row + j * piece : row + (j + 1) * piece, : high * chan] = lines.astype(bf16)
-
-    part[...] = jnp.zeros_like(part)
-    split(0, 7, dot(grad[: 7 * total], edge_in[: 7 * chan], NT))
-    row = 7 * piece
-    for first, high in ((7, 6), (19, 5)):
-        grad_plus = grad[first * total : (first + high) * total]
-        grad_minus = grad[(first + high) * total : (first + 2 * high) * total]
-        in_plus = edge_in[first * chan : (first + high) * chan]
-        in_minus = edge_in[(first + high) * chan : (first + 2 * high) * chan]
-        split(row, high, dot(grad_plus, in_plus, NT) + dot(grad_minus, in_minus, NT))
-        row += high * piece
-        split(row, high, dot(grad_minus, in_plus, NT) - dot(grad_plus, in_minus, NT))
-        row += high * piece
-
-    order = [d for d in range(pairs - 1, 0, -1)] + [0]
-    stage_one = []
-    for d in order:
-        q = lax.rem(mine + d, pairs)
-        copy = remote(
-            part.at[2 * q + (1 - core)], near.at[d], send1.at[d], recv1.at[d], "brick", sibling
-        )
-        copy.start()
-        stage_one.append(copy)
 
     gx[...] = jnp.zeros_like(gx)
 
     def back_block(i, carry):
         cols = pl.ds(pl.multiple_of(i * width, width), width)
-        back[: 7 * chan] = dot(wz[...], grad[: 7 * total, cols], NN)
-        for w, first, high in ((w1, 7, 6), (w2, 19, 5)):
-            low, middle, top = first, first + high, first + 2 * high
-            plus = grad[low * total : middle * total, cols]
-            minus = grad[middle * total : top * total, cols]
-            back[low * chan : middle * chan] = dot(w[0], plus, NN) + dot(w[1], minus, NN)
-            back[middle * chan : top * chan] = dot(w[0], minus, NN) - dot(w[1], plus, NN)
 
         def lanes_step(t, inner):
             near_at = pl.ds(pl.multiple_of(t * LANES, LANES), LANES)
@@ -263,7 +306,7 @@
                 full[c * chan : (c + 1) * chan, near_at] = tile.astype(bf16)
 
             unrotate_tile(
-                lambda r: back[r * chan : (r + 1) * chan, near_at],
+                lambda r: back[r * chan : (r + 1) * chan, at],
                 lambda k: wide[k : k + 1, at],
                 store,
             )
@@ -273,22 +316,7 @@
         gx[: coef * chan] += dot(full[...], at_src[:, cols], NT)
         return carry
 
-    lax.fori_loop(0, 1, back_block, 0)
-    stage_two = []
-    for copy, d in zip(stage_one, order):
-        copy.wait_recv()
-        q = lax.rem(mine + d, pairs)
-        both = part[2 * q + core].astype(f32) + near[d].astype(f32)
-        if d:
-            outgoing[d] = both.astype(bf16)
-            copy = remote(
-                outgoing.at[d], far.at[d], send2.at[d], recv2.at[d], "brick", 2 * q + core
-            )
-            copy.start()
-            stage_two.append(copy)
-        else:
-            sum_ref[...] = both
-    lax.fori_loop(1, slots // width, back_block, 0)
+    lax.fori_loop(0, slots // width, back_block, 0)
 
     groups = atoms // rim
     rows = chan // groups
@@ -308,8 +336,8 @@
     ]
     for copy in rims:
         copy.start()
-    for copy, d in zip(stage_two, order):
-        copy.wait_recv()
+    for d in range(1, pairs):
+        stage_two(0, d).wait_recv()
         sum_ref[...] += far[d].astype(f32)
     for copy in rims:
         copy.wait_recv()
@@ -326,9 +354,13 @@
             total_lines = total_lines + lines.reshape(coef + 1, rows, atoms)[:coef]
         gx_ref[:, q * rows : (q + 1) * rows, :] = total_lines
 
-    for copy in halos + stage_one + stage_two + rims:
+    for copy in halos + rims:
         copy.wait_send()
+    for d in range(1, pairs):
+        stage_two(0, d).wait_send()
     for s in range(shards):
+        stage_one(s).wait_send()
+
         @pl.when((z < shards - 1) & (s <= z))
         def _():
             up(s).wait_send()
@@ -362,29 +394,33 @@
         return pltpu.SemaphoreType.DMA((count,))
 
     whole = pl.BlockSpec(memory_space=pltpu.VMEM)
+    hbm = pl.BlockSpec(memory_space=pltpu.HBM)
     sums, grad_x = pl.pallas_call(
         functools.partial(fused_kernel, bricks, shards, chan, total, piece, rim, width),
         out_shape=(
             jax.ShapeDtypeStruct((rows, 2 * LANES), f32),
             jax.ShapeDtypeStruct((coef, chan, atoms), f32),
         ),
-        in_specs=[pl.BlockSpec(memory_space=pltpu.SMEM)] + [whole] * 9,
+        in_specs=[pl.BlockSpec(memory_space=pltpu.SMEM)] + [whole] * 3 + [hbm] * 6,
         out_specs=(whole, whole),
         scratch_shapes=[
+            vmem((entries, slots), bf16), vmem((7, 7, chan, total), bf16),
+            vmem((2, 6, 6, chan, total), bf16), vmem((2, 5, 5, chan, total), bf16),
             vmem((entries, slots), f32), vmem((entries, slots), f32),
             vmem((atoms, slots), bf16), vmem((2 * atoms, slots), bf16),
             vmem((shards, flat, atoms), bf16), vmem((flat, atoms), bf16),
             vmem((flat, atoms), bf16), vmem((flat, 2 * atoms), bf16),
-            vmem((flat, width), f32), vmem((29 * total, slots), bf16),
-            vmem((29 * chan, slots), bf16), vmem((7 * chan, 7 * total), bf16),
-            vmem((2, 6 * chan, 6 * total), bf16), vmem((2, 5 * chan, 5 * total), bf16),
-            vmem((29 * chan, width), f32), vmem((flat, width), bf16),
+            vmem((flat, width), f32), vmem((29 * chan, slots), bf16),
+            vmem((29 * chan, slots), bf16), vmem((shards, 7 * chan, 7 * chan), bf16),
+            vmem((2, shards, 6 * chan, 6 * chan), bf16),
+            vmem((2, shards, 5 * chan, 5 * chan), bf16),
+            vmem((29 * chan, slots), f32), vmem((flat, width), bf16),
             vmem((flat + chan, 2 * atoms), f32), vmem((bricks, rows, 2 * LANES), bf16),
             vmem((pairs, rows, 2 * LANES), bf16), vmem((pairs, rows, 2 * LANES), bf16),
             vmem((pairs, rows, 2 * LANES), bf16),
             vmem((packed, atoms), bf16), vmem((packed, atoms), bf16),
             vmem((packed, atoms), bf16), vmem((packed, atoms), bf16),
-            dma(shards), dma(shards), dma(shards), dma(2), dma(2),
+            dma(6), dma(shards), dma(shards), dma(shards), dma(2), dma(2),
             dma(pairs), dma(pairs), dma(pairs), dma(pairs), dma(2), dma(2),
         ],
         compiler_params=pltpu.CompilerParams(
@@ -624,6 +660,6 @@
         P(None, None, "chan", None, "brick"),
     )
     bricks, shards = mesh.shape["brick"], mesh.shape["chan"]
-    fits = bricks % 2 == 0 and bricks > 2 and (128 // bricks) % 16 == 0 and shards <= 4
+    fits = bricks == 2 * shards and bricks == 8
     chosen = kernel_body if fits else body
     return jax.shard_map(chosen, mesh=mesh, in_specs=in_specs, out_specs=out_specs, check_vma=False)

time: 77.1 us -> 76.5 us (level)
  the two profiles are of different devices: /device:TPU:0 before, /device:TPU:6 now
where the time goes in v1:
time: 76.5 us; the launch traced here: 76.1 us
  Pallas kernels  63.6 us (83%)
  local copies, waits for them, and re-layouts  10.9 us (14%)
  between operations  1.39 us (2%)
    pallas_call x1, Pallas kernels, kernel_body(): pl.pallas_call(functools.partial(fused_kernel, bricks, shards, chan, tota...  63.6 us
    unnamed x22, local copies, waits for them, and re-layouts  10.3 us

profile of v1, /device:TPU:6, one launch (start us, length us, event | category | flops | bytes accessed | tf_op | source)
XLA Modules:
  0.0 76.1 jit_solution(7150370057913224532)
XLA Ops:
  1.3 0.0 copy-start.8
  1.3 0.0 copy-start.7
  1.3 0.0 copy-start.6
  1.3 0.7 copy-done.8
  2.0 0.0 copy-done.7
  2.0 0.0 copy-done.6
  2.0 0.0 copy-start
  2.0 1.1 %copy-done = bf16[2,6,32,6,128]{4,2,3,1,0:T(8,128)(2,1)S(1)} copy-done((bf16[2,6,32,6,128]{4,2,3,1,0:T(8,128)(2,1)S(1)}, bf16[2,6,32,6,128]{4,2,3,1,0:T(8,128)(2,1)}, u32[]{:S(2)}) %copy-start) | copy-done | bytes 589848
  3.1 0.0 copy-start.1
  3.1 1.0 %copy-done.1 = bf16[235,1024]{1,0:T(8,128)(2,1)S(1)} copy-done((bf16[235,1024]{1,0:T(8,128)(2,1)S(1)}, bf16[235,1024]{1,0:T(8,128)(2,1)}, u32[]{:S(2)}) %copy-start.1) | copy-done | bytes 481304
  4.1 0.0 copy-start.2
  4.1 1.0 %copy-done.2 = bf16[2,5,32,5,128]{4,2,3,1,0:T(8,128)(2,1)S(1)} copy-done((bf16[2,5,32,5,128]{4,2,3,1,0:T(8,128)(2,1)S(1)}, bf16[2,5,32,5,128]{4,2,3,1,0:T(8,128)(2,1)}, u32[]{:S(2)}) %copy-start.2) | copy-done | bytes 409624
  5.1 0.0 copy-start.3
  5.1 1.0 %copy-done.3 = bf16[49,32,128]{2,1,0:T(8,128)(2,1)S(1)} copy-done((bf16[49,32,128]{2,1,0:T(8,128)(2,1)S(1)}, bf16[49,32,128]{2,1,0:T(8,128)(2,1)}, u32[]{:S(2)}) %copy-start.3) | copy-done | bytes 401432
  6.1 0.0 copy-start.4
  6.1 1.0 %copy-done.4 = bf16[49,32,128]{2,1,0:T(8,128)(2,1)S(1)} copy-done((bf16[49,32,128]{2,1,0:T(8,128)(2,1)S(1)}, bf16[49,32,128]{2,1,0:T(8,128)(2,1)}, u32[]{:S(2)}) %copy-start.4) | copy-done | bytes 401432
  7.1 0.0 copy-start.5
  7.1 1.0 %copy-done.5 = bf16[7,32,7,128]{3,1,2,0:T(8,128)(2,1)S(1)} copy-done((bf16[7,32,7,128]{3,1,2,0:T(8,128)(2,1)S(1)}, bf16[7,32,7,128]{3,1,2,0:T(8,128)(2,1)}, u32[]{:S(2)}) %copy-start.5) | copy-done | bytes 401432
  8.1 63.6 %fused.1 = (f32[464,256]{1,0:T(8,128)S(1)}, f32[49,32,128]{2,1,0:T(8,128)S(1)}) custom-call(s32[1]{0:T(128)S(6)} %copy.23.count_ref, s32[1,1024]{1,0:T(1,128)S(1)} %bitcast.26, s32[1,1024]{1,0:T(1,128)S(1)} %bitcast.27, f32[1,1024]{1,0:T(1,128)S(1)} %bitcast.28, bf16[235,1024]{1,0:T(8,128)(2,1)S(1)} %copy-done.1, bf16[1568,128]{1,0:T(8,128)(2,1)S(1)} %bitcast.23, ...), custom_call_target="tpu_custom_call" | custom-call | tf_op jit(solution)/shard_map/fused/pallas_call | solution.py:398
  71.7 0.1 reshape.44
  71.9 0.1 reshape.45
  72.0 0.1 pad_maximum_fusion
  72.1 0.9 %copy.20 = f32[2,6,32,6,16]{2,4,3,1,0:T(8,128)} copy(f32[2,6,32,6,16]{2,1,4,3,0:T(8,128)S(1)} %pad_maximum_fusion) | data formatting | bytes 294912
  73.1 0.1 reshape.46
  73.2 0.1 reshape.47
  73.3 0.1 pad_maximum_fusion.1
  73.4 0.8 %copy.21 = f32[2,5,32,5,16]{2,4,3,1,0:T(8,128)} copy(f32[2,5,32,5,16]{2,1,4,3,0:T(8,128)S(1)} %pad_maximum_fusion.1) | data formatting | bytes 204800
  74.2 0.1 reshape.43
  74.4 0.8 %copy.19 = f32[7,32,7,16]{1,3,2,0:T(8,128)} copy(f32[7,32,7,16]{1,0,3,2:T(8,128)S(1)} %bitcast.29) | data formatting | bytes 200704
  75.2 0.9 %copy.24 = f32[49,32,128]{2,1,0:T(8,128)} copy(f32[49,32,128]{2,1,0:T(8,128)S(1)} %get-tuple-element.20) | data formatting | bytes 1605632
  (3 shorter events, 0.0 us)
Async XLA Ops:
  1.3 0.7 copy-start.8
  1.3 0.7 copy-start.7
  1.3 0.7 copy-start.6
  2.0 1.1 %copy-start = (bf16[2,6,32,6,128]{4,2,3,1,0:T(8,128)(2,1)S(1)}, bf16[2,6,32,6,128]{4,2,3,1,0:T(8,128)(2,1)}, u32[]{:S(2)}) copy-start(bf16[2,6,32,6,128]{4,2,3,1,0:T(8,128)(2,1)} %param.18) | copy-start | bytes 1769476
  3.1 1.0 %copy-start.1 = (bf16[235,1024]{1,0:T(8,128)(2,1)S(1)}, bf16[235,1024]{1,0:T(8,128)(2,1)}, u32[]{:S(2)}) copy-start(bf16[235,1024]{1,0:T(8,128)(2,1)} %wig_ref.1) | copy-start | bytes 1443844
  4.1 1.0 %copy-start.2 = (bf16[2,5,32,5,128]{4,2,3,1,0:T(8,128)(2,1)S(1)}, bf16[2,5,32,5,128]{4,2,3,1,0:T(8,128)(2,1)}, u32[]{:S(2)}) copy-start(bf16[2,5,32,5,128]{4,2,3,1,0:T(8,128)(2,1)} %param.19) | copy-start | bytes 1228804
  5.1 1.0 %copy-start.3 = (bf16[49,32,128]{2,1,0:T(8,128)(2,1)S(1)}, bf16[49,32,128]{2,1,0:T(8,128)(2,1)}, u32[]{:S(2)}) copy-start(bf16[49,32,128]{2,1,0:T(8,128)(2,1)} %param.11) | copy-start | bytes 1204228
  6.1 1.0 %copy-start.4 = (bf16[49,32,128]{2,1,0:T(8,128)(2,1)S(1)}, bf16[49,32,128]{2,1,0:T(8,128)(2,1)}, u32[]{:S(2)}) copy-start(bf16[49,32,128]{2,1,0:T(8,128)(2,1)} %param.10) | copy-start | bytes 1204228
  7.1 1.0 %copy-start.5 = (bf16[7,32,7,128]{3,1,2,0:T(8,128)(2,1)S(1)}, bf16[7,32,7,128]{3,1,2,0:T(8,128)(2,1)}, u32[]{:S(2)}) copy-start(bf16[7,32,7,128]{3,1,2,0:T(8,128)(2,1)} %param.17) | copy-start | bytes 1204228

commit v2 on v1

--- a/solution.py
+++ b/solution.py
@@ -8,7 +8,7 @@
 from jax.sharding import PartitionSpec as P
 
 LANES = 128
-VMEM_BYTES = 48 * 1024 * 1024
+VMEM_BYTES = 63 * 1024 * 1024
 MESH = pl.DeviceIdType.MESH
 NT = (((1,), (1,)), ((), ()))
 NN = (((1,), (0,)), ((), ()))
@@ -174,7 +174,21 @@
 
     lane = lax.broadcasted_iota(jnp.int32, (1, atoms), 1)
 
-    def first_shard():
+    def arrival(s):
+        return remote(cot_ref, cot.at[s], send_up.at[s], recv_cot.at[s], "chan", z)
+
+    def forward(d):
+        @pl.when((z - d >= 0) & (z < shards - 1))
+        def _():
+            arrival(z - d).wait_recv()
+            up(z - d).start()
+
+        @pl.when((z + d < shards) & (z > 0))
+        def _():
+            arrival(z + d).wait_recv()
+            down(z + d).start()
+
+    def split_weights():
         for copy in copies[3:]:
             copy.wait()
         for kept, source, lead, high in (
@@ -189,6 +203,9 @@
                             lead + (s, slice(i * chan, (i + 1) * chan),
                                     slice(j * chan, (j + 1) * chan))
                         ] = tile[:, s * chan : (s + 1) * chan]
+        part[...] = jnp.zeros_like(part)
+
+    def rotate_inputs():
         copies[2].wait()
         for copy in halos:
             copy.wait_recv()
@@ -196,7 +213,6 @@
             lane < rim, x_next[...].astype(f32), x_prev[...].astype(f32)
         ).astype(bf16)
         rotate_all(lambda: ext[...], at_src, wide, edge_in, chan, 0)
-        part[...] = jnp.zeros_like(part)
 
     def stage_one(s):
         return remote(
@@ -255,34 +271,28 @@
     def distance_step(d, carry):
         low, high = z - d, z + d
 
-        @pl.when((d > 0) & (low >= 0))
-        def _():
-            down_in = remote(cot_ref, cot.at[low], send_up.at[low], recv_cot.at[low], "chan", z)
-            down_in.wait_recv()
-
-            @pl.when(z < shards - 1)
-            def _():
-                up(low).start()
-
-        @pl.when((d > 0) & (high < shards))
-        def _():
-            up_in = remote(cot_ref, cot.at[high], send_up.at[high], recv_cot.at[high], "chan", z)
-            up_in.wait_recv()
-
-            @pl.when(z > 0)
-            def _():
-                down(high).start()
-
         def side_step(side, inner):
             s = jnp.where(side == 0, low, high)
 
             @pl.when((s >= 0) & (s < shards) & (d + (1 - side) > 0))
             def _():
+                @pl.when((d > 0) & (z == jnp.where(side == 0, shards - 1, 0)))
+                def _():
+                    arrival(s).wait_recv()
+
                 rotate_all(lambda: cot[s], at_dst, scaled, grad, chan, 0)
 
                 @pl.when(d == 0)
                 def _():
-                    first_shard()
+                    split_weights()
+
+                @pl.when((side == 0) | (low < 0))
+                def _():
+                    forward(d + 1)
+
+                @pl.when(d == 0)
+                def _():
+                    rotate_inputs()
 
                 shard_products(s)
 

time: 76.5 us -> 62.7 us (0.82)
  Pallas kernels: 63.6 us -> 55.6 us
  local copies, waits for them, and re-layouts: 10.9 us -> 5.27 us
    pallas_call x1, Pallas kernels: 63.6 us -> 55.6 us  [kernel_body(): pl.pallas_call(functools.partial(fused_kernel, bricks, shards, chan, tota...]
    unnamed x22 -> x8, local copies, waits for them, and re-layouts: 10.3 us -> 3.71 us
    slice x3, local copies, waits for them, and re-layouts: 0.04 us -> 0.98 us  [columns_back(): block = sums[first:first + high * piece, :high * chan]]
where the time goes in v2:
time: 62.7 us; the launch traced here: 62.5 us
  Pallas kernels  55.6 us (89%)
  local copies, waits for them, and re-layouts  5.27 us (8%)
  between operations  1.36 us (2%)
    pallas_call x1, Pallas kernels, kernel_body(): pl.pallas_call(functools.partial(fused_kernel, bricks, shards, chan, tota...  55.6 us
    unnamed x8, local copies, waits for them, and re-layouts  3.71 us

profile of v2, /device:TPU:6, one launch (start us, length us, event | category | flops | bytes accessed | tf_op | source)
XLA Modules:
  0.0 62.5 jit_solution(710426430836266723)
XLA Ops:
  1.3 55.6 %fused.1 = (f32[464,256]{1,0:T(8,128)}, f32[49,32,128]{2,1,0:T(8,128)}) custom-call(s32[1]{0:T(128)S(6)} %copy.23.count_ref, s32[1,1024]{1,0:T(1,128)} %bitcast.31, s32[1,1024]{1,0:T(1,128)} %bitcast.32, f32[1,1024]{1,0:T(1,128)} %bitcast.33, bf16[235,1024]{1,0:T(8,128)(2,1)} %wig_ref.1, bf16[1568,128]{1,0:T(8,128)(2,1)} %bitcast.28, ...), custom_call_target="tpu_custom_call" | custom-call | tf_op jit(solution)/shard_map/fused/pallas_call | solution.py:408
  56.9 1.0 %fusion.1 = (f32[96,192]{1,0:T(8,128)S(1)}, f32[96,192]{1,0:T(8,128)S(1)}) fusion(f32[464,256]{1,0:T(8,128)} %get-tuple-element.7), kind=kLoop, calls=%fused_computation.3 | loop fusion | bytes 294912 | tf_op jit(solution)/shard_map/slice | solution.py:448
  57.9 0.1 reshape.44
  58.0 0.1 reshape.45
  58.1 0.1 pad_maximum_fusion
  58.3 0.0 copy-start.1
  58.3 0.9 %copy.20 = f32[2,6,32,6,16]{2,4,3,1,0:T(8,128)} copy(f32[2,6,32,6,16]{2,1,4,3,0:T(8,128)S(1)} %pad_maximum_fusion) | data formatting | bytes 294912
  59.2 0.1 copy-done.1
  59.3 0.1 reshape.46
  59.4 0.1 reshape.47
  59.5 0.1 pad_maximum_fusion.1
  59.6 0.8 %copy.21 = f32[2,5,32,5,16]{2,4,3,1,0:T(8,128)} copy(f32[2,5,32,5,16]{2,1,4,3,0:T(8,128)S(1)} %pad_maximum_fusion.1) | data formatting | bytes 204800
  60.4 0.0 copy-start
  60.5 0.1 reshape.43
  60.6 0.8 %copy.19 = f32[7,32,7,16]{1,3,2,0:T(8,128)} copy(f32[7,32,7,16]{1,0,3,2:T(8,128)S(1)} %bitcast.21) | data formatting | bytes 200704
  61.4 0.1 copy-done
  61.6 0.9 %copy.24 = f32[49,32,128]{2,1,0:T(8,128)} copy(f32[49,32,128]{2,1,0:T(8,128)S(1)} %copy-done) | data formatting | bytes 1605632
  (2 shorter events, 0.0 us)
Async XLA Ops:
  58.3 1.0 %copy-start.1 = (f32[464,256]{1,0:T(8,128)S(1)}, f32[464,256]{1,0:T(8,128)}, u32[]{:S(2)}) copy-start(f32[464,256]{1,0:T(8,128)} %get-tuple-element.7) | copy-start | bytes 1425412
  60.4 1.1 %copy-start = (f32[49,32,128]{2,1,0:T(8,128)S(1)}, f32[49,32,128]{2,1,0:T(8,128)}, u32[]{:S(2)}) copy-start(f32[49,32,128]{2,1,0:T(8,128)} %get-tuple-element.20) | copy-start | bytes 2408452

commit v3 on v2

--- a/solution.py
+++ b/solution.py
@@ -59,8 +59,8 @@
 def fused_kernel(
     bricks, shards, chan, total, piece, rim, width,
     count_ref, src_ref, dst_ref, scale_ref, wig_ref, cot_ref, x_ref, wz_ref, w1_ref, w2_ref,
-    sum_ref, gx_ref,
-    wig_in, wz_in, w1_in, w2_in,
+    zero_ref, one_ref, two_ref, gx_ref,
+    sum_ref, wig_in, wz_in, w1_in, w2_in,
     wide, scaled, at_dst, at_src, cot, x_next, x_prev, ext, gathered, grad, edge_in,
     wz, w1, w2, back, full, gx, part, near, far, outgoing, to_next, to_prev, from_next, from_prev,
     local, send_up, send_down, recv_cot, send_x, recv_x, send1, recv1, send2, recv2,
@@ -349,6 +349,12 @@
     for d in range(1, pairs):
         stage_two(0, d).wait_recv()
         sum_ref[...] += far[d].astype(f32)
+    zero_ref[...] = sum_ref[: 7 * piece, : 7 * chan]
+    for k in range(2):
+        low = (7 + 6 * k) * piece
+        one_ref[k] = sum_ref[low : low + 6 * piece, : 6 * chan]
+        low = (19 + 5 * k) * piece
+        two_ref[k] = sum_ref[low : low + 5 * piece, : 5 * chan]
     for copy in rims:
         copy.wait_recv()
     arrived = [from_prev[...].astype(f32), from_next[...].astype(f32)]
@@ -405,16 +411,18 @@
 
     whole = pl.BlockSpec(memory_space=pltpu.VMEM)
     hbm = pl.BlockSpec(memory_space=pltpu.HBM)
-    sums, grad_x = pl.pallas_call(
+    zero, one, two, grad_x = pl.pallas_call(
         functools.partial(fused_kernel, bricks, shards, chan, total, piece, rim, width),
         out_shape=(
-            jax.ShapeDtypeStruct((rows, 2 * LANES), f32),
+            jax.ShapeDtypeStruct((7 * piece, 7 * chan), f32),
+            jax.ShapeDtypeStruct((2, 6 * piece, 6 * chan), f32),
+            jax.ShapeDtypeStruct((2, 5 * piece, 5 * chan), f32),
             jax.ShapeDtypeStruct((coef, chan, atoms), f32),
         ),
         in_specs=[pl.BlockSpec(memory_space=pltpu.SMEM)] + [whole] * 3 + [hbm] * 6,
-        out_specs=(whole, whole),
+        out_specs=(whole, whole, whole, whole),
         scratch_shapes=[
-            vmem((entries, slots), bf16), vmem((7, 7, chan, total), bf16),
+            vmem((rows, 2 * LANES), f32), vmem((entries, slots), bf16), vmem((7, 7, chan, total), bf16),
             vmem((2, 6, 6, chan, total), bf16), vmem((2, 5, 5, chan, total), bf16),
             vmem((entries, slots), f32), vmem((entries, slots), f32),
             vmem((atoms, slots), bf16), vmem((2 * atoms, slots), bf16),
@@ -444,17 +452,12 @@
         w_one.transpose(0, 1, 3, 2, 4), w_two.transpose(0, 1, 3, 2, 4),
     )
 
-    def columns_back(first, high):
-        block = sums[first : first + high * piece, : high * chan]
-        return block.reshape(high, piece, high, chan).transpose(2, 3, 0, 1)
-
-    ends = [0, 7 * piece, 13 * piece, 19 * piece, 24 * piece]
-    return (
-        grad_x,
-        columns_back(ends[0], 7),
-        jnp.stack([columns_back(ends[1], 6), columns_back(ends[2], 6)]),
-        jnp.stack([columns_back(ends[3], 5), columns_back(ends[4], 5)]),
-    )
+    def columns_back(sums, high):
+        lead = sums.shape[:-2]
+        sums = sums.reshape(lead + (high, piece, high, chan))
+        return jnp.moveaxis(sums, (-2, -1), (-4, -3))
+
+    return (grad_x, columns_back(zero, 7), columns_back(one, 6), columns_back(two, 5))
 
 
 def padded(x, sides, width):

time: 62.7 us -> 62.4 us (level)
    slice x3 -> x0, local copies, waits for them, and re-layouts: 0.98 us -> none  [columns_back(): block = sums[first:first + high * piece, :high * chan]]
    reshape x5 -> x3, local copies, waits for them, and re-layouts: 0.59 us -> 1.37 us  [columns_back(): sums = sums.reshape(lead + (high, piece, high, chan))]
    unnamed x8 -> x10, local copies, waits for them, and re-layouts: 3.71 us -> 3.73 us
where the time goes in v3:
time: 62.4 us; the launch traced here: 62.1 us
  Pallas kernels  55.7 us (89%)
  local copies, waits for them, and re-layouts  5.1 us (8%)
  between operations  1.33 us (2%)
    pallas_call x1, Pallas kernels, kernel_body(): pl.pallas_call(functools.partial(fused_kernel, bricks, shards, chan, tota...  55.7 us
    unnamed x10, local copies, waits for them, and re-layouts  3.73 us
    reshape x3, local copies, waits for them, and re-layouts, columns_back(): sums = sums.reshape(lead + (high, piece, high, chan))  1.37 us

profile of v3, /device:TPU:6, one launch (start us, length us, event | category | flops | bytes accessed | tf_op | source)
XLA Modules:
  0.0 62.1 jit_solution(8183061147189321335)
XLA Ops:
  1.3 55.7 %fused.1 = (f32[112,224]{1,0:T(8,128)}, f32[2,96,192]{2,1,0:T(8,128)}, f32[2,80,160]{2,1,0:T(8,128)}, f32[49,32,128]{2,1,0:T(8,128)}) custom-call(s32[1]{0:T(128)S(6)} %copy.21.count_ref, s32[1,1024]{1,0:T(1,128)} %bitcast.19, s32[1,1024]{1,0:T(1,128)} %bitcast.20, f32[1,1024]{1,0:T(1,128)} %bitcast.21, bf16[235,1024]{1,0:T(8,128)(2,1)} %wig_ref.1, ...), custom_call_target="tpu_custom_call" | custom-call | tf_op jit(solution)/shard_map/fused/pallas_call | solution.py:414
  57.0 1.0 %reshape.37 = f32[7,16,7,32]{3,2,1,0:T(8,128)S(1)} reshape(f32[112,224]{1,0:T(8,128)} %get-tuple-element.9) | data formatting | bytes 200704 | tf_op jit(solution)/shard_map/reshape | solution.py:457
  58.0 0.0 copy-start.1
  58.0 0.8 %copy.17 = f32[7,32,7,16]{1,3,2,0:T(8,128)} copy(f32[7,32,7,16]{1,0,3,2:T(8,128)S(1)} %bitcast.13) | data formatting | bytes 200704
  58.9 0.1 copy-done.1
  59.0 0.2 reshape.38
  59.2 0.0 copy-start.2
  59.2 0.9 %copy.18 = f32[2,6,32,6,16]{2,4,3,1,0:T(8,128)} copy(f32[2,6,32,6,16]{2,1,4,3,0:T(8,128)S(1)} %bitcast.11) | data formatting | bytes 294912
  60.1 0.0 copy-done.2
  60.1 0.0 copy-start
  60.1 0.1 reshape.39
  60.2 0.8 %copy.19 = f32[2,5,32,5,16]{2,4,3,1,0:T(8,128)} copy(f32[2,5,32,5,16]{2,1,4,3,0:T(8,128)S(1)} %bitcast.12) | data formatting | bytes 204800
  61.1 0.2 copy-done
  61.2 0.9 %copy.22 = f32[49,32,128]{2,1,0:T(8,128)} copy(f32[49,32,128]{2,1,0:T(8,128)S(1)} %copy-done) | data formatting | bytes 1605632
Async XLA Ops:
  58.0 0.9 %copy-start.1 = (f32[2,96,192]{2,1,0:T(8,128)S(1)}, f32[2,96,192]{2,1,0:T(8,128)}, u32[]{:S(2)}) copy-start(f32[2,96,192]{2,1,0:T(8,128)} %get-tuple-element.10) | copy-start | bytes 442372
  59.2 0.9 %copy-start.2 = (f32[2,80,160]{2,1,0:T(8,128)S(1)}, f32[2,80,160]{2,1,0:T(8,128)}, u32[]{:S(2)}) copy-start(f32[2,80,160]{2,1,0:T(8,128)} %get-tuple-element.11) | copy-start | bytes 307204
  60.1 1.1 %copy-start = (f32[49,32,128]{2,1,0:T(8,128)S(1)}, f32[49,32,128]{2,1,0:T(8,128)}, u32[]{:S(2)}) copy-start(f32[49,32,128]{2,1,0:T(8,128)} %get-tuple-element.20) | copy-start | bytes 2408452
